TPU v7x, 32 devices: a whole 2x2x4 slice. The times are simulated.
32 devices in a mesh: along: 8 (over z, x), across: 4 (over y, core).
Axes of the slice: x: 2, y: 2, z: 4, core: 2. Of those that a mesh axis runs over, the one named last changes fastest.
Arguments:
- features: bfloat16 [32768, 256], P(('along', 'across')), may hold values from -6 to 6
- adj_tiles: bfloat16 [256, 4, 128, 128], P(('along', 'across')), may hold values from -0.25 to 0.25
- adj_index: int32 [256, 4], P(('along', 'across')), may hold values from 0 to 11, as said below
- adj_count: int32 [256], P(('along', 'across')), may hold values from 2 to 4, as said below
- bnd_index: int32 [4096], P(('along', 'across')), may hold values from 0 to 1023
- pool_index: int32 [32768], P(('along', 'across')), may hold values from 0 to 15
- w_msg: bfloat16 [256, 256], replicated, may hold values from -0.375 to 0.375
- w_update: bfloat16 [512, 256], replicated, may hold values from -0.25 to 0.25
- w_coarse: bfloat16 [256, 256], replicated, may hold values from -0.375 to 0.375
- cotangent: bfloat16 [32768, 256], P(('along', 'across')), may hold values from -0.3125 to 0.3125
Outputs:
- updated: bfloat16 [32768, 256], P(('along', 'across'))
- weight_grads: float32 [131072], P(('along', 'across'))
Inputs may be any that keep to these rules, and one draw needn't show every extreme that they name: `adj_index`: indices 0 to 7 name the partition's own blocks, 8 to 11 the four boundary tiles in the order of the sources. Slot 0 of every block names the block itself. Slots from adj_count on are ignored. Some block has all 4 slots live.
All inputs are finite; a program needn't handle non-finite values.
Results may differ from a plain program's by a relative error of at most 0.0062.
Values may be sent and summed in bfloat16 or wider, within the bound.
A program may use at most 64 MiB of HBM per device.

v0:
```python
import jax
import jax.numpy as jnp
from jax import lax
from jax.sharding import PartitionSpec as P

NC_DEV = 4


eps = 1e-05


def extended(block, sides, width):
    for axis, dim in sides:
        count = lax.axis_size(axis)
        forward = [(i, i + 1) for i in range(count - 1)]
        backward = [(target, source) for source, target in forward]
        low = lax.ppermute(
            lax.slice_in_dim(block, block.shape[dim] - width, None, axis=dim), axis, forward
        )
        high = lax.ppermute(lax.slice_in_dim(block, 0, width, axis=dim), axis, backward)
        block = jnp.concatenate([low, block, high], axis=dim)
    return block


def normalize(values):
    center = values - jnp.mean(values, axis=-1, keepdims=True)
    inverse = lax.rsqrt(jnp.mean(center * center, axis=-1, keepdims=True) + eps)
    return (center * inverse, inverse)


def silu_slope(values):
    logistic = jax.nn.sigmoid(values)
    return logistic * (1.0 + values * (1.0 - logistic))


def transposed_times(operand, second, precision=None):
    return lax.dot_general(
        operand,
        second,
        (((0,), (0,)), ((), ())),
        precision=precision,
        preferred_element_type=jnp.float32,
    )


def times_transposed(operand, second):
    return lax.dot_general(
        operand, second, (((1,), (1,)), ((), ())), preferred_element_type=jnp.float32
    )


def coarse_forward(pooled, w_coarse):
    coarse_norm, inverse = normalize(pooled)
    coarse = coarse_norm.astype(jnp.bfloat16)
    coarse_pre = jnp.dot(coarse, w_coarse, preferred_element_type=jnp.float32)
    return (coarse_norm, inverse, coarse, coarse_pre, jax.nn.silu(coarse_pre).astype(jnp.bfloat16))


def coarse_backward(coarse_cot, coarse_norm, inverse, coarse_pre, w_coarse):
    coarse_delta = (coarse_cot * silu_slope(coarse_pre)).astype(jnp.bfloat16)
    coarse_back = times_transposed(coarse_delta, w_coarse)
    mean_one = jnp.mean(coarse_back, axis=-1, keepdims=True)
    mean_two = jnp.mean(coarse_back * coarse_norm, axis=-1, keepdims=True)
    return (coarse_delta, inverse * (coarse_back - mean_one - coarse_norm * mean_two))


def local(
    features,
    adj_tiles,
    adj_index,
    adj_count,
    bnd_index,
    pool_index,
    w_msg,
    w_update,
    w_coarse,
    cotangent,
):
    feature_count = features.shape[1]
    blocks = adj_tiles.shape[0]
    slot_count = adj_tiles.shape[1]
    tile_rows = adj_tiles.shape[2]
    inputs = features.astype(jnp.float32)
    normed, _ = normalize(inputs)
    scaled = normed.astype(jnp.bfloat16)
    rim_rows = scaled[bnd_index]
    padded = extended(rim_rows[None, None], (("along", 0), ("across", 1)), 1)
    halo_tiles = jnp.stack([padded[0, 1], padded[2, 1], padded[1, 0], padded[1, 2]])
    sources = jnp.concatenate(
        [scaled.reshape(blocks, tile_rows, feature_count), halo_tiles], axis=0
    )
    messages = jnp.dot(
        sources.reshape(-1, feature_count), w_msg, preferred_element_type=jnp.float32
    )
    messages = messages.astype(jnp.bfloat16).reshape(sources.shape)
    live_slots = jnp.arange(slot_count)[None, :] < adj_count[:, None]
    masked_tiles = jnp.where(live_slots[:, :, None, None], adj_tiles, jnp.zeros((), jnp.bfloat16))
    aggregated = jnp.einsum(
        "bkij,bkjh->bih", masked_tiles, messages[adj_index], preferred_element_type=jnp.float32
    )
    aggregated = aggregated.astype(jnp.bfloat16).reshape(-1, feature_count)
    summed_scaled = jnp.einsum(
        "bkij,bkjh->bih", masked_tiles, sources[adj_index], preferred_element_type=jnp.float32
    )
    summed_scaled = summed_scaled.astype(jnp.bfloat16).reshape(-1, feature_count)
    w_first = w_update[:feature_count]
    w_second = w_update[feature_count:]
    update_pre = jnp.dot(scaled, w_first, preferred_element_type=jnp.float32) + jnp.dot(
        aggregated, w_second, preferred_element_type=jnp.float32
    )
    hidden_one = inputs + jax.nn.silu(update_pre)
    coarse_count = NC_DEV * lax.axis_size("across")
    assign_float = (pool_index[:, None] == jnp.arange(coarse_count)[None, :]).astype(jnp.float32)
    assign_bits = assign_float.astype(jnp.bfloat16)
    pooled_part = transposed_times(assign_float, hidden_one, lax.Precision.HIGHEST)
    cot_part = transposed_times(assign_bits, cotangent)
    pooled, coarse_cot = lax.psum((pooled_part, cot_part), "across")
    coarse_norm, inverse, coarse, coarse_pre, coarse_out = coarse_forward(pooled, w_coarse)
    hidden_two = hidden_one + jnp.dot(assign_bits, coarse_out, preferred_element_type=jnp.float32)
    coarse_delta, pooled_delta = coarse_backward(
        coarse_cot, coarse_norm, inverse, coarse_pre, w_coarse
    )
    start = lax.axis_index("across") * NC_DEV
    own_coarse = lax.dynamic_slice_in_dim(coarse, start, NC_DEV, 0)
    own_coarse_delta = lax.dynamic_slice_in_dim(coarse_delta, start, NC_DEV, 0)
    coarse_grad = transposed_times(own_coarse, own_coarse_delta)
    hidden_delta = cotangent.astype(jnp.float32) + jnp.dot(
        assign_float,
        pooled_delta,
        precision=lax.Precision.HIGHEST,
        preferred_element_type=jnp.float32,
    )
    update_delta = (hidden_delta * silu_slope(update_pre)).astype(jnp.bfloat16)
    aggregated_delta = times_transposed(update_delta, w_second).astype(jnp.bfloat16)
    message_grad = transposed_times(summed_scaled, aggregated_delta)
    grad_terms = jnp.concatenate([message_grad.reshape(-1), coarse_grad.reshape(-1)])
    partial_grads = lax.psum_scatter(grad_terms, "along", scatter_dimension=0, tiled=True)
    weight_grads = lax.psum_scatter(partial_grads, "across", scatter_dimension=0, tiled=True)
    return (hidden_two.astype(jnp.bfloat16), weight_grads)


def solution(mesh):
    return jax.shard_map(
        local,
        mesh=mesh,
        in_specs=(
            P(("along", "across"), None),
            P(("along", "across"), None, None, None),
            P(("along", "across"), None),
            P(("along", "across")),
            P(("along", "across")),
            P(("along", "across")),
            P(),
            P(),
            P(),
            P(("along", "across"), None),
        ),
        out_specs=(P(("along", "across"), None), P(("along", "across"))),
        check_vma=False,
    )
```

profile of v0, /device:TPU:0, one launch (start us, length us, event | category | flops | bytes accessed | tf_op | source)
XLA Modules:
  0.0 176.5 jit_solution(7514516907137922514)
XLA Ops:
  7.2 0.0 copy-start
  7.2 0.0 copy-start.13
  7.2 0.0 copy-start.12
  7.2 0.0 copy-start.14
  7.2 0.0 copy-start.8
  7.2 0.0 all-reduce.6.cloned.1.call-start
  7.3 1.3 convert_reduce_fusion
  8.6 1.4 fusion.9
  10.0 0.0 copy-start.6
  10.0 0.0 copy-start.10
  10.1 1.4 fusion.10
  11.5 0.0 copy-done.13
  11.5 0.8 gather_fusion
  12.4 4.8 %collective-permute-start = (bf16[1,1,128,256]{3,2,1,0:T(8,128)(2,1)S(1)}, bf16[1,1,128,256]{3,2,1,0:T(8,128)(2,1)S(1)}, u32[]{:S(2)}, u32[]{:S(2)}) collective-permute-start(bf16[1,1,128,256]{3,2,1,0:T(8,128)(2,1)S(1)} %bitcast.59), channel_id=1, source_target_pairs={{0,4},{4,8},{8,12},{12,16},{16,20},{20,24},{24,28},{1,5},{5,9},{9,... | collective-permute-start | bytes 196616 | tf_op jit(solution)/shard_map/ppermute | solution.py:17
  17.2 1.3 collective-permute-start.1
  18.6 0.1 copy.14
  18.7 0.1 reshape.96
  18.8 0.0 copy-done.14
  18.8 0.6 iota_compare_fusion.3
  19.4 0.0 copy-done.8
  19.4 0.3 fusion.19
  19.7 0.0 copy-done.6
  19.7 0.4 fusion.14
  20.1 0.0 collective-permute-done
  20.2 3.2 %collective-permute-done.1 = bf16[1,1,128,256]{3,2,1,0:T(8,128)(2,1)S(1)} collective-permute-done((bf16[1,1,128,256]{3,2,1,0:T(8,128)(2,1)S(1)}, bf16[1,1,128,256]{3,2,1,0:T(8,128)(2,1)S(1)}, u32[]{:S(2)}, u32[]{:S(2)}) %collective-permute-start.1) | collective-permute-done | bytes 65568 | tf_op jit(solution)/shard_map/ppermute | solution.py:20
  23.4 1.3 collective-permute-start.2
  24.7 1.3 collective-permute-start.3
  26.1 0.0 collective-permute-done.2
  26.1 3.7 %collective-permute-done.3 = bf16[3,1,128,256]{3,2,1,0:T(8,128)(2,1)S(1)} collective-permute-done((bf16[3,1,128,256]{3,2,1,0:T(8,128)(2,1)S(1)}, bf16[3,1,128,256]{3,2,1,0:T(8,128)(2,1)S(1)}, u32[]{:S(2)}, u32[]{:S(2)}) %collective-permute-start.3) | collective-permute-done | bytes 196640 | tf_op jit(solution)/shard_map/ppermute | solution.py:20
  29.8 2.0 %gather_fusion.2 = bf16[32,128,256]{2,1,0:T(8,128)(2,1)} fusion(bf16[12,128,256]{2,1,0:T(8,128)(2,1)S(1)} %fusion.24, s32[1024]{0:T(1024)S(1)} %pad_clamp_fusion), kind=kCustom, calls=%fused_computation.2 | custom fusion | bytes 4194432 | tf_op jit(solution)/shard_map/gather | solution.py:103
  31.8 0.4 convolution_convert_fusion
  32.2 0.0 copy-start.16
  32.2 2.0 %gather_fusion.1 = bf16[32,128,256]{2,1,0:T(8,128)(2,1)} fusion(bf16[12,128,256]{2,1,0:T(8,128)(2,1)S(1)} %bitcast.52, s32[1024]{0:T(1024)S(1)} %pad_clamp_fusion), kind=kCustom, calls=%fused_computation.1 | custom fusion | bytes 4194432 | tf_op jit(solution)/shard_map/gather | solution.py:99
  34.2 2.4 %fusion.2 = bf16[8,128,256]{2,1,0:T(8,128)(2,1)S(1)} fusion(bf16[8,4,128,256]{3,2,1,0:T(8,128)(2,1)} %bitcast.55, bf16[8,4,128,128]{3,2,1,0:T(8,128)(2,1)} %param.11, pred[8,4]{1,0:T(8,128)(4,1)S(1)} %copy-done.16), kind=kOutput, calls=%fused_computation.15 | convolution fusion | flops 269221888 | bytes 3670048 | tf_op jit(solution)/shard_map/bkij,bkjh->bih/dot_general | solution.py:98
  36.6 0.0 copy-start.11
  36.7 0.3 convolution_add_fusion.1
  37.0 1.0 copy-done.3
  38.0 0.0 copy-start.17
  38.0 1.0 fusion.11
  38.9 14.3 %all-reduce.2 = (f32[16,256]{1,0:T(8,128)S(1)}, f32[16,256]{1,0:T(8,128)S(1)}) all-reduce(f32[16,256]{1,0:T(8,128)S(1)} %fusion.11, f32[16,256]{1,0:T(8,128)S(1)} %fusion.14), channel_id=1, replica_groups=mesh['along'=8,'across'=4] {'across'}, use_global_device_ids=true, to_apply=%region_2.3 | all-reduce | flops 8192 | bytes 65536 | tf_op jit(solution)/shard_map/psum | solution.py:117
  53.3 0.1 reduce_sum.56
  53.4 0.2 multiply_reduce_fusion.1
  53.6 0.1 fusion.30
  53.7 0.2 multiply_convert_fusion
  53.9 0.0 copy-start.7
  53.9 0.3 fusion.42
  54.2 2.7 %fusion.3 = bf16[8,128,256]{2,1,0:T(8,128)(2,1)} fusion(bf16[8,4,128,256]{3,2,1,0:T(8,128)(2,1)S(1)} %bitcast.54, bf16[8,4,128,128]{3,2,1,0:T(8,128)(2,1)} %param.11, pred[8,4]{1,0:T(8,128)(4,1)S(1)} %copy-done.17), kind=kOutput, calls=%fused_computation.16 | convolution fusion | flops 269221888 | bytes 3670048 | tf_op jit(solution)/shard_map/bkij,bkjh->bih/dot_general | solution.py:102
  56.9 0.0 copy-start.15
  56.9 1.6 fusion.4
  58.5 1.8 fusion.8
  60.3 0.1 copy.17
  60.5 0.2 convolution_bitcast_fusion.2
  60.7 0.1 copy.18
  60.8 0.8 pad_maximum_fusion
  61.7 0.0 all-reduce.6.cloned.1.call-update
  61.7 0.0 all-reduce.8.cloned.1.call-start
  61.8 0.6 dynamic-slice
  62.3 0.6 dynamic-slice.2
  64.2 71.3 %all-reduce.6.cloned.1.call-done = f32[131072]{0:T(1024)} async-done(((f32[131072]{0:T(1024)}), f32[131072]{0:T(1024)}) %all-reduce.6.cloned.1.call-update) | async-done | bytes 524304
  135.5 1.5 dynamic-slice.1
  137.0 0.0 all-reduce.8.cloned.1.call-update
  137.0 1.3 fusion.1
  138.3 30.0 %all-reduce.8.cloned.1.call-done = f32[16384]{0:T(1024)} async-done(((f32[16384]{0:T(1024)}), f32[16384]{0:T(1024)}) %all-reduce.8.cloned.1.call-update) | async-done | bytes 65552
  168.3 1.3 dynamic-slice.3
  (38 shorter events, 0.2 us)
Async XLA Ops:
  7.2 24.7 %copy-start = (bf16[256,256]{1,0:T(8,128)(2,1)S(1)}, bf16[256,256]{1,0:T(8,128)(2,1)}, u32[]{:S(2)}) copy-start(bf16[256,256]{1,0:T(8,128)(2,1)} %param.16) | copy-start | bytes 393220
  7.2 4.3 %copy-start.13 = (s32[128]{0:T(128)S(1)}, s32[128]{0:T(128)}, u32[]{:S(2)}) copy-start(s32[128]{0:T(128)} %param.14) | copy-start | bytes 1540
  7.2 11.4 %copy-start.12 = (s32[8,4]{0,1:T(4,128)S(1)}, s32[8,4]{0,1:T(4,128)}, u32[]{:S(2)}) copy-start(s32[8,4]{0,1:T(4,128)} %param.12) | copy-start | bytes 388
  7.2 11.6 %copy-start.14 = (s32[8]{0:T(128)S(1)}, s32[8]{0:T(128)}, u32[]{:S(2)}) copy-start(s32[8]{0:T(128)} %param.13) | copy-start | bytes 100
  7.2 12.2 %copy-start.8 = (bf16[512,256]{1,0:T(8,128)(2,1)S(1)}, bf16[512,256]{1,0:T(8,128)(2,1)}, u32[]{:S(2)}) copy-start(bf16[512,256]{1,0:T(8,128)(2,1)} %param.17) | copy-start | bytes 786436
  7.2 128.3 %all-reduce.6.cloned.1.call-start = ((), (), s32[]{:S(2)}) async-start(), calls=%async_computation | async-start | bytes 1048576
  10.0 9.7 %copy-start.6 = (bf16[1024,256]{1,0:T(8,128)(2,1)S(1)}, bf16[1024,256]{1,0:T(8,128)(2,1)}, u32[]{:S(2)}) copy-start(bf16[1024,256]{1,0:T(8,128)(2,1)} %param.19) | copy-start | bytes 1572868
  10.0 9.7 %copy-start.10 = (s32[1024]{0:T(1024)S(1)}, s32[1024]{0:T(1024)}, u32[]{:S(2)}) copy-start(s32[1024]{0:T(1024)} %param.15) | copy-start | bytes 12292
  12.4 7.8 %collective-permute-start = (bf16[1,1,128,256]{3,2,1,0:T(8,128)(2,1)S(1)}, bf16[1,1,128,256]{3,2,1,0:T(8,128)(2,1)S(1)}, u32[]{:S(2)}, u32[]{:S(2)}) collective-permute-start(bf16[1,1,128,256]{3,2,1,0:T(8,128)(2,1)S(1)} %bitcast.59), channel_id=1, source_target_pairs={{0,4},{4,8},{8,12},{12,16},{16,20},{20,24},{24,28},{1,5},{5,9},{9,... | collective-permute-start | bytes 196616 | tf_op jit(solution)/shard_map/ppermute | solution.py:17
  17.2 6.2 %collective-permute-start.1 = (bf16[1,1,128,256]{3,2,1,0:T(8,128)(2,1)S(1)}, bf16[1,1,128,256]{3,2,1,0:T(8,128)(2,1)S(1)}, u32[]{:S(2)}, u32[]{:S(2)}) collective-permute-start(bf16[1,1,128,256]{3,2,1,0:T(8,128)(2,1)S(1)} %bitcast.60), channel_id=1, source_target_pairs={{4,0},{8,4},{12,8},{16,12},{20,16},{24,20},{28,24},{5,1},{9,5},{13... | collective-permute-start | bytes 196616 | tf_op jit(solution)/shard_map/ppermute | solution.py:20
  23.4 2.6 %collective-permute-start.2 = (bf16[3,1,128,256]{3,2,1,0:T(8,128)(2,1)S(1)}, bf16[3,1,128,256]{3,2,1,0:T(8,128)(2,1)S(1)}, u32[]{:S(2)}, u32[]{:S(2)}) collective-permute-start(bf16[3,1,128,256]{3,2,1,0:T(8,128)(2,1)S(1)} %pad_maximum_fusion.1), channel_id=1, source_target_pairs={{0,1},{1,2},{2,3},{4,5},{5,6},{6,7},{8,9},{9,10},{10,11},{12,13},{... | collective-permute-start | bytes 589832 | tf_op jit(solution)/shard_map/ppermute | solution.py:17
  24.7 5.1 %collective-permute-start.3 = (bf16[3,1,128,256]{3,2,1,0:T(8,128)(2,1)S(1)}, bf16[3,1,128,256]{3,2,1,0:T(8,128)(2,1)S(1)}, u32[]{:S(2)}, u32[]{:S(2)}) collective-permute-start(bf16[3,1,128,256]{3,2,1,0:T(8,128)(2,1)S(1)} %pad_maximum_fusion.1), channel_id=1, source_target_pairs={{1,0},{2,1},{3,2},{5,4},{6,5},{7,6},{9,8},{10,9},{11,10},{13,12},{... | collective-permute-start | bytes 589832 | tf_op jit(solution)/shard_map/ppermute | solution.py:20
  32.2 2.0 %copy-start.16 = (pred[8,4]{1,0:T(8,128)(4,1)S(1)}, pred[8,4]{1,0:T(8,128)(4,1)}, u32[]{:S(2)}) copy-start(pred[8,4]{1,0:T(8,128)(4,1)} %iota_compare_fusion.3) | copy-start | bytes 100
  36.6 1.3 copy-start.1
  36.6 1.3 copy-start.11
  37.0 1.0 copy-start.3
  38.0 15.7 %copy-start.9 = (bf16[256,256]{1,0:T(8,128)(2,1)S(1)}, bf16[256,256]{1,0:T(8,128)(2,1)}, u32[]{:S(2)}) copy-start(bf16[256,256]{1,0:T(8,128)(2,1)} %param.18) | copy-start | bytes 393220
  38.0 16.2 %copy-start.2 = (bf16[32,128,256]{2,1,0:T(8,128)(2,1)S(1)}, bf16[32,128,256]{2,1,0:T(8,128)(2,1)}, u32[]{:S(2)}) copy-start(bf16[32,128,256]{2,1,0:T(8,128)(2,1)} %gather_fusion.2) | copy-start | bytes 6291460
  38.0 16.2 %copy-start.17 = (pred[8,4]{1,0:T(8,128)(4,1)S(1)}, pred[8,4]{1,0:T(8,128)(4,1)}, u32[]{:S(2)}) copy-start(pred[8,4]{1,0:T(8,128)(4,1)} %iota_compare_fusion.3) | copy-start | bytes 100
  53.9 3.0 %copy-start.4 = (f32[1024,256]{1,0:T(8,128)S(1)}, f32[1024,256]{1,0:T(8,128)}, u32[]{:S(2)}) copy-start(f32[1024,256]{1,0:T(8,128)} %copy-done.3) | copy-start | bytes 3145732
  53.9 3.0 %copy-start.7 = (bf16[1024,256]{1,0:T(8,128)(2,1)S(1)}, bf16[1024,256]{1,0:T(8,128)(2,1)}, u32[]{:S(2)}) copy-start(bf16[1024,256]{1,0:T(8,128)(2,1)} %param.19) | copy-start | bytes 1572868
  56.9 1.7 copy-start.15
  58.5 3.2 %copy-start.19 = (u32[32]{0:T(128)S(1)}, u32[32]{0:T(128)}, u32[]{:S(2)}) copy-start(u32[32]{0:T(128)} %constant.44) | copy-start | bytes 388
  58.5 3.8 %copy-start.18 = (u32[32]{0:T(128)S(1)}, u32[32]{0:T(128)}, u32[]{:S(2)}) copy-start(u32[32]{0:T(128)} %constant.48) | copy-start | bytes 388
  58.5 78.5 %copy-start.5 = (f32[1024,256]{1,0:T(8,128)S(1)}, f32[1024,256]{1,0:T(8,128)}, u32[]{:S(2)}) copy-start(f32[1024,256]{1,0:T(8,128)} %copy-done.3) | copy-start | bytes 3145732
  61.7 106.6 %all-reduce.8.cloned.1.call-start = ((), (), s32[]{:S(2)}) async-start(), calls=%async_computation.1 | async-start | bytes 131072
Sparse Core Ops, SparseCore 0:
  61.8 73.6 all-reduce.5
  137.9 30.3 all-reduce.7
where the time goes:
time: 177 us; the launch traced here: 176 us
  waiting for transfers between devices  108 us (61%)
  between operations  15.7 us (9%)
  blocking collectives  14.3 us (8%)
  matrix products  12.8 us (7%)
  local copies, waits for them, and re-layouts  10.4 us (6%)
  starting transfers between devices  8.81 us (5%)
  other arithmetic  6.09 us (3%)
    unnamed x4, waiting for transfers between devices  101 us
    psum x1, blocking collectives, local(): pooled, coarse_cot = lax.psum((pooled_part, cot_part), 'across')  14.3 us
    ppermute x2, waiting for transfers between devices, extended(): lax.ppermute(lax.slice_in_dim(block, 0, width, axis=dim), axis, backward)  6.96 us
    ppermute x2, starting transfers between devices, extended(): lax.ppermute(lax.slice_in_dim(block, block.shape[dim] - width, None, axis...  6.15 us
    unnamed x50, local copies, waits for them, and re-layouts  5.37 us
  transfers between devices with their start and end apart: 6, of which 4 were waited for; matrix products, arithmetic and copies ran while one was open for 2% of the time, Pallas kernels for 0%

commit v1 on v0

--- a/solution.py
+++ b/solution.py
@@ -1,6 +1,10 @@
+import functools
+
 import jax
 import jax.numpy as jnp
 from jax import lax
+from jax.experimental import pallas as pl
+from jax.experimental.pallas import tpu as pltpu
 from jax.sharding import PartitionSpec as P
 
 NC_DEV = 4
@@ -64,7 +68,7 @@
     return (coarse_delta, inverse * (coarse_back - mean_one - coarse_norm * mean_two))
 
 
-def local(
+def plain_layer(
     features,
     adj_tiles,
     adj_index,
@@ -139,9 +143,466 @@
     return (hidden_two.astype(jnp.bfloat16), weight_grads)
 
 
+MESH = pl.DeviceIdType.MESH
+f32 = jnp.float32
+bf16 = jnp.bfloat16
+
+
+def split(values):
+    high = values.astype(bf16)
+    return high, (values - high.astype(f32)).astype(bf16)
+
+
+def dot(first, second):
+    return jnp.dot(first, second, preferred_element_type=f32)
+
+
+def sigmoid(values):
+    return 0.5 * jnp.tanh(0.5 * values) + 0.5
+
+
+def layer_kernel(
+    n_along,
+    n_across,
+    adj_index,
+    adj_count,
+    bnd_row,
+    pool_row,
+    features_hbm,
+    adj_hbm,
+    w_msg_hbm,
+    w_update_hbm,
+    w_coarse_hbm,
+    cotangent_hbm,
+    updated_hbm,
+    grads,
+    features,
+    adj,
+    w_msg,
+    w_update,
+    w_coarse,
+    cotangent,
+    sources,
+    rim,
+    w_joined,
+    pre,
+    hidden,
+    slope,
+    summed,
+    summed_t,
+    update_delta,
+    updated,
+    pool_all,
+    cot_all,
+    pack,
+    pack_all,
+    coarse_grad,
+    total,
+    part,
+    part_all,
+    second,
+    second_all,
+    own_chunk,
+    in_sem,
+    out_sem,
+    halo_send,
+    halo_recv,
+    pool_send,
+    pool_recv,
+    cot_send,
+    cot_recv,
+    pack_send,
+    pack_recv,
+    part_send,
+    part_recv,
+    second_send,
+    second_recv,
+):
+    a = lax.axis_index("along")
+    c = lax.axis_index("across")
+    half = n_along // 2
+    nodes, width = features.shape
+    blocks, slots, tile, _ = adj.shape
+    coarse_count = NC_DEV * n_across
+    chunk = grads.shape[0]
+
+    loads = [
+        pltpu.make_async_copy(source, target, in_sem.at[i])
+        for i, (source, target) in enumerate(
+            (
+                (features_hbm, features),
+                (cotangent_hbm, cotangent),
+                (w_update_hbm, w_update),
+                (w_msg_hbm, w_msg),
+                (adj_hbm, adj),
+                (w_coarse_hbm, w_coarse),
+            )
+        )
+    ]
+    for load in loads:
+        load.start()
+
+    barrier = pltpu.get_barrier_semaphore()
+    across_peers = [lax.rem(c + d, n_across) for d in range(1, n_across)]
+    along_peers = [lax.rem(a + d, n_along) for d in range(1, n_along)]
+    for peer in across_peers:
+        pl.semaphore_signal(barrier, inc=1, device_id=(a, peer), device_id_type=MESH)
+    for peer in along_peers:
+        pl.semaphore_signal(barrier, inc=1, device_id=(peer, c), device_id_type=MESH)
+
+    def remote(source, target, send, recv, device):
+        return pltpu.make_async_remote_copy(
+            src_ref=source,
+            dst_ref=target,
+            send_sem=send,
+            recv_sem=recv,
+            device_id=device,
+            device_id_type=MESH,
+        )
+
+    loads[0].wait()
+    for b in range(blocks):
+        x = features[b * tile : (b + 1) * tile, :].astype(f32)
+        sources[b] = normalize(x)[0].astype(bf16)
+    local_rows = sources[0:blocks].reshape(nodes, width)
+    rim_pick = (lax.broadcasted_iota(jnp.int32, (nodes, tile), 0) == bnd_row[...]).astype(f32)
+    rim[...] = transposed_times(rim_pick.astype(bf16), local_rows).astype(bf16)
+
+    pl.semaphore_wait(barrier, n_across - 1 + n_along - 1)
+
+    sides = (
+        (a < n_along - 1, (a + 1, c), a > 0),
+        (a > 0, (a - 1, c), a < n_along - 1),
+        (c < n_across - 1, (a, c + 1), c > 0),
+        (c > 0, (a, c - 1), c < n_across - 1),
+    )
+
+    def halo(side, device):
+        return remote(
+            rim, sources.at[blocks + side], halo_send.at[side], halo_recv.at[side], device
+        )
+
+    for side, (has_target, device, has_source) in enumerate(sides):
+
+        @pl.when(has_target)
+        def _(side=side, device=device):
+            halo(side, device).start()
+
+        @pl.when(jnp.logical_not(has_source))
+        def _(side=side):
+            sources[blocks + side] = jnp.zeros((tile, width), bf16)
+
+    pool_pick = (
+        lax.broadcasted_iota(jnp.int32, (coarse_count, nodes), 0) == pool_row[...]
+    ).astype(f32).astype(bf16)
+    loads[1].wait()
+    cot_all[c] = dot(pool_pick, cotangent[...])
+    cot_copies = [
+        remote(cot_all.at[c], cot_all.at[c], cot_send.at[d], cot_recv.at[c], (a, peer))
+        for d, peer in enumerate(across_peers)
+    ]
+    for copy in cot_copies:
+        copy.start()
+
+    loads[2].wait()
+    loads[3].wait()
+    w_first = w_update[0:width, :]
+    w_second = w_update[width : 2 * width, :]
+    w_joined[...] = dot(w_msg[...], w_second).astype(bf16)
+    for b in range(blocks):
+        pre[b * tile : (b + 1) * tile, :] = dot(sources[b], w_first)
+
+    loads[4].wait()
+    for side, (has_target, device, has_source) in enumerate(sides):
+
+        @pl.when(has_source)
+        def _(side=side):
+            halo(side, (a, c)).wait_recv()
+
+    pooled = jnp.zeros((coarse_count, width), f32)
+    for b in range(blocks):
+        rows = slice(b * tile, (b + 1) * tile)
+        gathered = jnp.concatenate([sources[adj_index[b, k]] for k in range(slots)], axis=0)
+        weights = jnp.concatenate(
+            [
+                adj[b, k]
+                * jnp.where(k < adj_count[b], 1.0, 0.0).astype(bf16)
+                for k in range(slots)
+            ],
+            axis=1,
+        )
+        block_sum = dot(weights, gathered).astype(bf16)
+        summed[rows, :] = block_sum
+        v = pre[rows, :] + dot(block_sum, w_joined[...])
+        s = sigmoid(v)
+        slope[rows, :] = s * (1.0 + v * (1.0 - s))
+        h = features[rows, :].astype(f32) + v * s
+        hidden[rows, :] = h
+        high, low = split(h)
+        pick = pool_pick[:, rows]
+        pooled += dot(pick, high) + dot(pick, low)
+    pool_all[c] = pooled
+    pool_copies = [
+        remote(pool_all.at[c], pool_all.at[c], pool_send.at[d], pool_recv.at[c], (a, peer))
+        for d, peer in enumerate(across_peers)
+    ]
+    for copy in pool_copies:
+        copy.start()
+
+    for b in range(blocks):
+        rows = slice(b * tile, (b + 1) * tile)
+        summed_t[:, rows] = summed[rows, :].T
+    loads[5].wait()
+
+    for peer in across_peers:
+        remote(
+            cot_all.at[peer], cot_all.at[peer], cot_send.at[0], cot_recv.at[peer], (a, c)
+        ).wait_recv()
+        remote(
+            pool_all.at[peer], pool_all.at[peer], pool_send.at[0], pool_recv.at[peer], (a, c)
+        ).wait_recv()
+    pooled, coarse_cot = pool_all[0], cot_all[0]
+    for i in range(1, n_across):
+        pooled, coarse_cot = pooled + pool_all[i], coarse_cot + cot_all[i]
+
+    coarse_norm, inverse = normalize(pooled)
+    coarse = coarse_norm.astype(bf16)
+    coarse_pre = dot(coarse, w_coarse[...])
+    s = sigmoid(coarse_pre)
+    coarse_out = (coarse_pre * s).astype(bf16)
+    coarse_delta = (coarse_cot * (s * (1.0 + coarse_pre * (1.0 - s)))).astype(bf16)
+    pack[0:coarse_count, :] = coarse
+    pack[coarse_count : 2 * coarse_count, :] = coarse_delta
+
+    def send_pack(target):
+        return remote(pack, pack_all.at[a], pack_send.at[target - half], pack_recv.at[a], (target, c))
+
+    for target in range(half, n_along):
+
+        @pl.when(a != target)
+        def _(target=target):
+            send_pack(target).start()
+
+    coarse_back = times_transposed(coarse_delta, w_coarse[...])
+    mean_one = jnp.mean(coarse_back, axis=-1, keepdims=True)
+    mean_two = jnp.mean(coarse_back * coarse_norm, axis=-1, keepdims=True)
+    pooled_delta = inverse * (coarse_back - mean_one - coarse_norm * mean_two)
+    delta_parts = jnp.concatenate(split(pooled_delta), axis=0)
+    twice_pick = jnp.concatenate([pool_pick, pool_pick], axis=0)
+
+    for b in range(blocks):
+        rows = slice(b * tile, (b + 1) * tile)
+        spread = transposed_times(twice_pick[:, rows], delta_parts)
+        hidden_delta = cotangent[rows, :].astype(f32) + spread
+        update_delta[rows, :] = (hidden_delta * slope[rows, :]).astype(bf16)
+    total[...] = dot(summed_t[...], update_delta[...])
+
+    for i in range(half):
+        for j in range(n_across):
+            start = (i * n_across + j) * chunk
+            part[j, i] = total[start : start + chunk, :].astype(bf16)
+
+    def send_part(i, d, peer):
+        return remote(
+            part.at[peer, i], part_all.at[c, i], part_send.at[d, i], part_recv.at[c, i], (a, peer)
+        )
+
+    for i in reversed(range(half)):
+        for d, peer in enumerate(across_peers):
+            send_part(i, d, peer).start()
+
+    for b in range(blocks):
+        rows = slice(b * tile, (b + 1) * tile)
+        spread = transposed_times(pool_pick[:, rows], coarse_out)
+        updated[rows, :] = (hidden[rows, :] + spread).astype(bf16)
+    store = pltpu.make_async_copy(updated, updated_hbm, out_sem.at[0])
+    store.start()
+
+    def send_second(i):
+        return remote(
+            second.at[i], second_all.at[a], second_send.at[i], second_recv.at[a], (i, c)
+        )
+
+    for i in reversed(range(half)):
+        start = pl.multiple_of((i * n_across + c) * chunk, chunk)
+        chunk_sum = total[pl.ds(start, chunk), :]
+        for peer in across_peers:
+            remote(
+                part.at[peer, i], part_all.at[peer, i], part_send.at[0, i], part_recv.at[peer, i], (a, c)
+            ).wait_recv()
+            chunk_sum = chunk_sum + part_all[peer, i].astype(f32)
+
+        @pl.when(a == i)
+        def _(chunk_sum=chunk_sum):
+            own_chunk[...] = chunk_sum
+
+        @pl.when(a != i)
+        def _(chunk_sum=chunk_sum, i=i):
+            second[i] = chunk_sum.astype(bf16)
+            send_second(i).start()
+
+    @pl.when(a < half)
+    def _():
+        chunk_sum = own_chunk[...]
+        for peer in along_peers:
+            remote(
+                second.at[0], second_all.at[peer], second_send.at[0], second_recv.at[peer], (a, c)
+            ).wait_recv()
+            chunk_sum = chunk_sum + second_all[peer].astype(f32)
+        high, low = split(chunk_sum)
+        both = times_transposed(jnp.concatenate([high, low], axis=0), w_second)
+        grads[...] = both[0:chunk, :] + both[chunk : 2 * chunk, :]
+
+    @pl.when(a >= half)
+    def _():
+        pack_all[a] = pack[...]
+        for peer in along_peers:
+            remote(
+                pack, pack_all.at[peer], pack_send.at[0], pack_recv.at[peer], (a, c)
+            ).wait_recv()
+        rows = n_along * coarse_count
+        all_coarse = pack_all[:, 0:coarse_count, :].reshape(rows, width)
+        all_delta = pack_all[:, coarse_count : 2 * coarse_count, :].reshape(rows, width)
+        coarse_grad[...] = transposed_times(all_coarse, all_delta)
+        start = pl.multiple_of(((a - half) * n_across + c) * chunk, chunk)
+        grads[...] = coarse_grad[pl.ds(start, chunk), :]
+
+    for side, (has_target, device, has_source) in enumerate(sides):
+
+        @pl.when(has_target)
+        def _(side=side, device=device):
+            halo(side, device).wait_send()
+
+    for copy in cot_copies + pool_copies:
+        copy.wait_send()
+    for target in range(half, n_along):
+
+        @pl.when(a != target)
+        def _(target=target):
+            send_pack(target).wait_send()
+
+    for i in range(half):
+        for d, peer in enumerate(across_peers):
+            send_part(i, d, peer).wait_send()
+
+        @pl.when(a != i)
+        def _(i=i):
+            send_second(i).wait_send()
+
+    store.wait()
+
+
+def fused_layer(
+    n_along,
+    n_across,
+    chunk,
+    features,
+    adj_tiles,
+    adj_index,
+    adj_count,
+    bnd_index,
+    pool_index,
+    w_msg,
+    w_update,
+    w_coarse,
+    cotangent,
+):
+    nodes, width = features.shape
+    blocks, slots, tile, _ = adj_tiles.shape
+    half = n_along // 2
+    coarse_count = NC_DEV * n_across
+    vmem = pltpu.VMEM
+    dma = pltpu.SemaphoreType.DMA
+    smem_spec = pl.BlockSpec(memory_space=pltpu.SMEM)
+    vmem_spec = pl.BlockSpec(memory_space=pltpu.VMEM)
+    any_spec = pl.BlockSpec(memory_space=pl.ANY)
+    updated, grads = pl.pallas_call(
+        functools.partial(layer_kernel, n_along, n_across),
+        name="mesh_layer",
+        out_shape=(
+            jax.ShapeDtypeStruct((nodes, width), bf16),
+            jax.ShapeDtypeStruct((chunk, width), f32),
+        ),
+        in_specs=[smem_spec] * 2 + [vmem_spec] * 2 + [any_spec] * 6,
+        out_specs=(any_spec, vmem_spec),
+        scratch_shapes=[
+            vmem((nodes, width), bf16),
+            vmem(adj_tiles.shape, bf16),
+            vmem(w_msg.shape, bf16),
+            vmem(w_update.shape, bf16),
+            vmem(w_coarse.shape, bf16),
+            vmem((nodes, width), bf16),
+            vmem((blocks + 4, tile, width), bf16),
+            vmem((tile, width), bf16),
+            vmem((width, width), bf16),
+            vmem((nodes, width), f32),
+            vmem((nodes, width), f32),
+            vmem((nodes, width), f32),
+            vmem((nodes, width), bf16),
+            vmem((width, nodes), bf16),
+            vmem((nodes, width), bf16),
+            vmem((nodes, width), bf16),
+            vmem((n_across, coarse_count, width), f32),
+            vmem((n_across, coarse_count, width), f32),
+            vmem((2 * coarse_count, width), bf16),
+            vmem((n_along, 2 * coarse_count, width), bf16),
+            vmem((width, width), f32),
+            vmem((width, width), f32),
+            vmem((n_across, half, chunk, width), bf16),
+            vmem((n_across, half, chunk, width), bf16),
+            vmem((half, chunk, width), bf16),
+            vmem((n_along, chunk, width), bf16),
+            vmem((chunk, width), f32),
+            dma((6,)),
+            dma((1,)),
+            dma((4,)),
+            dma((4,)),
+            dma((n_across,)),
+            dma((n_across,)),
+            dma((n_across,)),
+            dma((n_across,)),
+            dma((half,)),
+            dma((n_along,)),
+            dma((n_across, half)),
+            dma((n_across, half)),
+            dma((half,)),
+            dma((n_along,)),
+        ],
+        compiler_params=pltpu.CompilerParams(
+            collective_id=0, has_side_effects=True, vmem_limit_bytes=40 * 2**20
+        ),
+        cost_estimate=pl.CostEstimate(
+            flops=2 * nodes * width * (slots * tile + 5 * width),
+            bytes_accessed=4 * 2**20,
+            transcendentals=nodes * width,
+        ),
+    )(
+        adj_index,
+        adj_count,
+        bnd_index.reshape(1, tile),
+        pool_index.reshape(1, nodes),
+        features,
+        adj_tiles,
+        w_msg,
+        w_update,
+        w_coarse,
+        cotangent,
+    )
+    return updated, grads.reshape(-1)
+
+
+def layer(axes, features, adj_tiles, *others):
+    n_along, n_across = axes["along"], axes["across"]
+    width = features.shape[1]
+    chunk = 2 * width // (n_along * n_across)
+    if n_along % 2 == 0 and chunk and chunk % 16 == 0:
+        return fused_layer(n_along, n_across, chunk, features, adj_tiles, *others)
+    return plain_layer(features, adj_tiles, *others)
+
+
 def solution(mesh):
     return jax.shard_map(
-        local,
+        functools.partial(layer, dict(mesh.shape)),
         mesh=mesh,
         in_specs=(
             P(("along", "across"), None),

time: 177 us -> 34.3 us (0.19)
  waiting for transfers between devices: 108 us -> 0 us
  Pallas kernels: 0 us -> 24.5 us
  between operations: 15.7 us -> 0.67 us
  blocking collectives: 14.3 us -> 0 us
  matrix products: 12.8 us -> 0 us
  starting transfers between devices: 8.81 us -> 0 us
  other arithmetic: 6.09 us -> 0 us
    unnamed x4 -> x0, waiting for transfers between devices: 101 us -> none
    pallas_call x0 -> x1, Pallas kernels: none -> 24.5 us  [fused_layer(): pl.pallas_call(functools.partial(layer_kernel, n_along, n_across), name='...]
    psum x1 -> x0, blocking collectives: 14.3 us -> none  [local(): pooled, coarse_cot = lax.psum((pooled_part, cot_part), 'across')]
    dot_general x13 -> x0, matrix products: 12.8 us -> none  [the longest x4 3.34 us: transposed_times(): lax.dot_general(operand, second, (((0,), (0,)), ((), ())), precision=prec...]
    ppermute x4 -> x0, starting transfers between devices: 8.73 us -> none  [the longest x2 6.15 us: extended(): lax.ppermute(lax.slice_in_dim(block, block.shape[dim] - width, None, axis...]
    ppermute x4 -> x0, waiting for transfers between devices: 6.96 us -> none  [the longest x2 6.96 us: extended(): lax.ppermute(lax.slice_in_dim(block, 0, width, axis=dim), axis, backward)]
    gather x3 -> x0, local copies, waits for them, and re-layouts: 4.86 us -> none  [the longest x1 2.03 us: local(): sources[adj_index]]
    unnamed x50 -> x23, local copies, waits for them, and re-layouts: 5.37 us -> 8.81 us
  transfers between devices with their start and end apart: 6 -> 0, of which waited for: 4 -> 0; matrix products, arithmetic and copies ran while one was open for 2% -> 0% of each run, Pallas kernels for 0% -> 0%
where the time goes in v1:
time: 34.3 us; the launch traced here: 33.9 us
  Pallas kernels  24.5 us (71%)
  local copies, waits for them, and re-layouts  8.81 us (26%)
  between operations  0.67 us (2%)
    pallas_call x1, Pallas kernels, fused_layer(): pl.pallas_call(functools.partial(layer_kernel, n_along, n_across), name='...  24.5 us
    unnamed x23, local copies, waits for them, and re-layouts  8.81 us

profile of v1, /device:TPU:0, one launch (start us, length us, event | category | flops | bytes accessed | tf_op | source)
XLA Modules:
  0.0 33.9 jit_solution(7502734031446130856)
XLA Ops:
  0.6 0.0 copy-start.9
  0.6 0.0 copy-start.6
  0.7 0.7 %copy-done.9 = s32[8,4]{0,1:T(4,128)S(1)} copy-done((s32[8,4]{0,1:T(4,128)S(1)}, s32[8,4]{0,1:T(4,128)}, u32[]{:S(2)}) %copy-start.9) | copy-done | bytes 152
  1.3 0.0 copy-start.7
  1.3 0.0 copy-start.8
  1.3 0.1 copy.12.adj_index
  1.4 0.0 copy-done.6
  1.4 0.6 %copy-done.7 = s32[8]{0:T(128)S(1)} copy-done((s32[8]{0:T(128)S(1)}, s32[8]{0:T(128)}, u32[]{:S(2)}) %copy-start.7) | copy-done | bytes 56
  2.0 0.0 copy-done.8
  2.0 0.0 copy-start
  2.0 1.2 %copy-done = bf16[8,4,128,128]{3,2,1,0:T(8,128)(2,1)S(1)} copy-done((bf16[8,4,128,128]{3,2,1,0:T(8,128)(2,1)S(1)}, bf16[8,4,128,128]{3,2,1,0:T(8,128)(2,1)}, u32[]{:S(2)}) %copy-start) | copy-done | bytes 1048600
  3.2 0.0 copy-start.1
  3.2 1.0 %copy-done.1 = bf16[1024,256]{1,0:T(8,128)(2,1)S(1)} copy-done((bf16[1024,256]{1,0:T(8,128)(2,1)S(1)}, bf16[1024,256]{1,0:T(8,128)(2,1)}, u32[]{:S(2)}) %copy-start.1) | copy-done | bytes 524312
  4.3 0.0 copy-start.2
  4.3 1.0 %copy-done.2 = bf16[1024,256]{1,0:T(8,128)(2,1)S(1)} copy-done((bf16[1024,256]{1,0:T(8,128)(2,1)S(1)}, bf16[1024,256]{1,0:T(8,128)(2,1)}, u32[]{:S(2)}) %copy-start.2) | copy-done | bytes 524312
  5.3 0.0 copy-start.3
  5.3 0.9 %copy-done.3 = bf16[512,256]{1,0:T(8,128)(2,1)S(1)} copy-done((bf16[512,256]{1,0:T(8,128)(2,1)S(1)}, bf16[512,256]{1,0:T(8,128)(2,1)}, u32[]{:S(2)}) %copy-start.3) | copy-done | bytes 262168
  6.2 0.0 copy-start.4
  6.2 0.9 %copy-done.4 = bf16[256,256]{1,0:T(8,128)(2,1)S(1)} copy-done((bf16[256,256]{1,0:T(8,128)(2,1)S(1)}, bf16[256,256]{1,0:T(8,128)(2,1)}, u32[]{:S(2)}) %copy-start.4) | copy-done | bytes 131096
  7.2 0.0 copy-start.5
  7.2 0.9 %copy-done.5 = bf16[256,256]{1,0:T(8,128)(2,1)S(1)} copy-done((bf16[256,256]{1,0:T(8,128)(2,1)S(1)}, bf16[256,256]{1,0:T(8,128)(2,1)}, u32[]{:S(2)}) %copy-start.5) | copy-done | bytes 131096
  8.1 24.5 %mesh_layer.1 = (bf16[1024,256]{1,0:T(8,128)(2,1)S(1)}, f32[16,256]{1,0:T(8,128)S(1)}) custom-call(s32[8,4]{1,0:T(8,128)S(1)} %copy.12.adj_index, s32[8]{0:T(128)S(1)} %copy-done.7, s32[1,128]{1,0:T(1,128)S(1)} %bitcast.6, s32[1,1024]{1,0:T(1,128)S(1)} %bitcast.5, bf16[1024,256]{1,0:T(8,128)(2,1)S(1)} %copy-done.1, bf16[8,4,128,128]{3,2,1,0:T(8,128)(2,1)S(1)} %copy-done, ...), custom_call_target="tpu_custom_call" | custom-call | flops 939524096 | bytes 4194304 | tf_op jit(solution)/shard_map/mesh_layer/pallas_call | solution.py:519
  32.5 0.6 %copy.13 = f32[2,2,8,128]{3,1,2,0:T(2,128)} copy(f32[2,2,8,128]{3,2,1,0:T(8,128)S(1)} %bitcast.4) | data formatting | bytes 32768
  33.1 0.8 %copy.15 = bf16[1024,256]{1,0:T(8,128)(2,1)} copy(bf16[1024,256]{1,0:T(8,128)(2,1)S(1)} %get-tuple-element.8) | data formatting | bytes 1048576
Async XLA Ops:
  0.6 0.7 %copy-start.9 = (s32[8,4]{0,1:T(4,128)S(1)}, s32[8,4]{0,1:T(4,128)}, u32[]{:S(2)}) copy-start(s32[8,4]{0,1:T(4,128)} %param.12) | copy-start | bytes 388
  0.6 0.8 %copy-start.6 = (s32[1024]{0:T(1024)S(1)}, s32[1024]{0:T(1024)}, u32[]{:S(2)}) copy-start(s32[1024]{0:T(1024)} %param.15) | copy-start | bytes 12292
  1.3 0.7 %copy-start.7 = (s32[8]{0:T(128)S(1)}, s32[8]{0:T(128)}, u32[]{:S(2)}) copy-start(s32[8]{0:T(128)} %adj_count.1) | copy-start | bytes 100
  1.3 0.7 %copy-start.8 = (s32[128]{0:T(128)S(1)}, s32[128]{0:T(128)}, u32[]{:S(2)}) copy-start(s32[128]{0:T(128)} %param.14) | copy-start | bytes 1540
  2.0 1.2 %copy-start = (bf16[8,4,128,128]{3,2,1,0:T(8,128)(2,1)S(1)}, bf16[8,4,128,128]{3,2,1,0:T(8,128)(2,1)}, u32[]{:S(2)}) copy-start(bf16[8,4,128,128]{3,2,1,0:T(8,128)(2,1)} %adj_hbm.1) | copy-start | bytes 3145732
  3.2 1.0 %copy-start.1 = (bf16[1024,256]{1,0:T(8,128)(2,1)S(1)}, bf16[1024,256]{1,0:T(8,128)(2,1)}, u32[]{:S(2)}) copy-start(bf16[1024,256]{1,0:T(8,128)(2,1)} %features_hbm.1) | copy-start | bytes 1572868
  4.3 1.0 %copy-start.2 = (bf16[1024,256]{1,0:T(8,128)(2,1)S(1)}, bf16[1024,256]{1,0:T(8,128)(2,1)}, u32[]{:S(2)}) copy-start(bf16[1024,256]{1,0:T(8,128)(2,1)} %cotangent_hbm.1) | copy-start | bytes 1572868
  5.3 0.9 %copy-start.3 = (bf16[512,256]{1,0:T(8,128)(2,1)S(1)}, bf16[512,256]{1,0:T(8,128)(2,1)}, u32[]{:S(2)}) copy-start(bf16[512,256]{1,0:T(8,128)(2,1)} %w_update_hbm.1) | copy-start | bytes 786436
  6.2 0.9 %copy-start.4 = (bf16[256,256]{1,0:T(8,128)(2,1)S(1)}, bf16[256,256]{1,0:T(8,128)(2,1)}, u32[]{:S(2)}) copy-start(bf16[256,256]{1,0:T(8,128)(2,1)} %w_msg_hbm.1) | copy-start | bytes 393220
  7.2 0.9 %copy-start.5 = (bf16[256,256]{1,0:T(8,128)(2,1)S(1)}, bf16[256,256]{1,0:T(8,128)(2,1)}, u32[]{:S(2)}) copy-start(bf16[256,256]{1,0:T(8,128)(2,1)} %w_coarse_hbm.1) | copy-start | bytes 393220

commit v2 on v1

--- a/solution.py
+++ b/solution.py
@@ -164,10 +164,10 @@
 def layer_kernel(
     n_along,
     n_across,
-    adj_index,
-    adj_count,
-    bnd_row,
-    pool_row,
+    index_hbm,
+    count_hbm,
+    bnd_hbm,
+    pool_hbm,
     features_hbm,
     adj_hbm,
     w_msg_hbm,
@@ -176,6 +176,10 @@
     cotangent_hbm,
     updated_hbm,
     grads,
+    adj_index,
+    adj_count,
+    bnd_row,
+    pool_row,
     features,
     adj,
     w_msg,
@@ -224,16 +228,26 @@
     nodes, width = features.shape
     blocks, slots, tile, _ = adj.shape
     coarse_count = NC_DEV * n_across
-    chunk = grads.shape[0]
+    chunk = own_chunk.shape[0]
+
+    def put_grads(values):
+        lanes = grads.shape[1]
+        parts = width // lanes
+        for i in range(parts):
+            grads[pl.ds(i, chunk, stride=parts), :] = values[:, i * lanes : (i + 1) * lanes]
 
     loads = [
         pltpu.make_async_copy(source, target, in_sem.at[i])
         for i, (source, target) in enumerate(
             (
                 (features_hbm, features),
+                (bnd_hbm, bnd_row),
+                (pool_hbm, pool_row),
                 (cotangent_hbm, cotangent),
                 (w_update_hbm, w_update),
                 (w_msg_hbm, w_msg),
+                (index_hbm, adj_index),
+                (count_hbm, adj_count),
                 (adj_hbm, adj),
                 (w_coarse_hbm, w_coarse),
             )
@@ -265,6 +279,7 @@
         x = features[b * tile : (b + 1) * tile, :].astype(f32)
         sources[b] = normalize(x)[0].astype(bf16)
     local_rows = sources[0:blocks].reshape(nodes, width)
+    loads[1].wait()
     rim_pick = (lax.broadcasted_iota(jnp.int32, (nodes, tile), 0) == bnd_row[...]).astype(f32)
     rim[...] = transposed_times(rim_pick.astype(bf16), local_rows).astype(bf16)
 
@@ -292,10 +307,11 @@
         def _(side=side):
             sources[blocks + side] = jnp.zeros((tile, width), bf16)
 
+    loads[2].wait()
     pool_pick = (
         lax.broadcasted_iota(jnp.int32, (coarse_count, nodes), 0) == pool_row[...]
     ).astype(f32).astype(bf16)
-    loads[1].wait()
+    loads[3].wait()
     cot_all[c] = dot(pool_pick, cotangent[...])
     cot_copies = [
         remote(cot_all.at[c], cot_all.at[c], cot_send.at[d], cot_recv.at[c], (a, peer))
@@ -304,15 +320,16 @@
     for copy in cot_copies:
         copy.start()
 
-    loads[2].wait()
-    loads[3].wait()
+    loads[4].wait()
+    loads[5].wait()
     w_first = w_update[0:width, :]
     w_second = w_update[width : 2 * width, :]
     w_joined[...] = dot(w_msg[...], w_second).astype(bf16)
     for b in range(blocks):
         pre[b * tile : (b + 1) * tile, :] = dot(sources[b], w_first)
 
-    loads[4].wait()
+    for load in loads[6:9]:
+        load.wait()
     for side, (has_target, device, has_source) in enumerate(sides):
 
         @pl.when(has_source)
@@ -322,11 +339,11 @@
     pooled = jnp.zeros((coarse_count, width), f32)
     for b in range(blocks):
         rows = slice(b * tile, (b + 1) * tile)
-        gathered = jnp.concatenate([sources[adj_index[b, k]] for k in range(slots)], axis=0)
+        gathered = jnp.concatenate([sources[adj_index[k, b]] for k in range(slots)], axis=0)
         weights = jnp.concatenate(
             [
                 adj[b, k]
-                * jnp.where(k < adj_count[b], 1.0, 0.0).astype(bf16)
+                * jnp.where(k < adj_count[0, b], 1.0, 0.0).astype(bf16)
                 for k in range(slots)
             ],
             axis=1,
@@ -352,7 +369,7 @@
     for b in range(blocks):
         rows = slice(b * tile, (b + 1) * tile)
         summed_t[:, rows] = summed[rows, :].T
-    loads[5].wait()
+    loads[9].wait()
 
     for peer in across_peers:
         remote(
@@ -451,7 +468,7 @@
             chunk_sum = chunk_sum + second_all[peer].astype(f32)
         high, low = split(chunk_sum)
         both = times_transposed(jnp.concatenate([high, low], axis=0), w_second)
-        grads[...] = both[0:chunk, :] + both[chunk : 2 * chunk, :]
+        put_grads(both[0:chunk, :] + both[chunk : 2 * chunk, :])
 
     @pl.when(a >= half)
     def _():
@@ -465,7 +482,7 @@
         all_delta = pack_all[:, coarse_count : 2 * coarse_count, :].reshape(rows, width)
         coarse_grad[...] = transposed_times(all_coarse, all_delta)
         start = pl.multiple_of(((a - half) * n_across + c) * chunk, chunk)
-        grads[...] = coarse_grad[pl.ds(start, chunk), :]
+        put_grads(coarse_grad[pl.ds(start, chunk), :])
 
     for side, (has_target, device, has_source) in enumerate(sides):
 
@@ -513,7 +530,7 @@
     coarse_count = NC_DEV * n_across
     vmem = pltpu.VMEM
     dma = pltpu.SemaphoreType.DMA
-    smem_spec = pl.BlockSpec(memory_space=pltpu.SMEM)
+    hbm_spec = pl.BlockSpec(memory_space=pltpu.HBM)
     vmem_spec = pl.BlockSpec(memory_space=pltpu.VMEM)
     any_spec = pl.BlockSpec(memory_space=pl.ANY)
     updated, grads = pl.pallas_call(
@@ -521,11 +538,15 @@
         name="mesh_layer",
         out_shape=(
             jax.ShapeDtypeStruct((nodes, width), bf16),
-            jax.ShapeDtypeStruct((chunk, width), f32),
+            jax.ShapeDtypeStruct((chunk * width // 128, 128), f32),
         ),
-        in_specs=[smem_spec] * 2 + [vmem_spec] * 2 + [any_spec] * 6,
+        in_specs=[hbm_spec] * 10,
         out_specs=(any_spec, vmem_spec),
         scratch_shapes=[
+            pltpu.SMEM((slots, blocks), jnp.int32),
+            pltpu.SMEM((1, blocks), jnp.int32),
+            vmem((1, tile), jnp.int32),
+            vmem((1, nodes), jnp.int32),
             vmem((nodes, width), bf16),
             vmem(adj_tiles.shape, bf16),
             vmem(w_msg.shape, bf16),
@@ -553,7 +574,7 @@
             vmem((half, chunk, width), bf16),
             vmem((n_along, chunk, width), bf16),
             vmem((chunk, width), f32),
-            dma((6,)),
+            dma((10,)),
             dma((1,)),
             dma((4,)),
             dma((4,)),
@@ -569,7 +590,7 @@
             dma((n_along,)),
         ],
         compiler_params=pltpu.CompilerParams(
-            collective_id=0, has_side_effects=True, vmem_limit_bytes=40 * 2**20
+            collective_id=0, has_side_effects=True, vmem_limit_bytes=60 * 2**20
         ),
         cost_estimate=pl.CostEstimate(
             flops=2 * nodes * width * (slots * tile + 5 * width),
@@ -577,8 +598,8 @@
             transcendentals=nodes * width,
         ),
     )(
-        adj_index,
-        adj_count,
+        adj_index.T,
+        adj_count.reshape(1, blocks),
         bnd_index.reshape(1, tile),
         pool_index.reshape(1, nodes),
         features,

time: 34.3 us -> 27.4 us (0.80)
  local copies, waits for them, and re-layouts: 8.81 us -> 2.48 us
  Pallas kernels: 24.5 us -> 24.1 us
    unnamed x23 -> x4, local copies, waits for them, and re-layouts: 8.81 us -> 2.48 us
    pallas_call x1, Pallas kernels: 24.5 us -> 24.1 us  [fused_layer(): pl.pallas_call(functools.partial(layer_kernel, n_along, n_across), name='...]
where the time goes in v2:
time: 27.4 us; the launch traced here: 27.2 us
  Pallas kernels  24.1 us (88%)
  local copies, waits for them, and re-layouts  2.48 us (9%)
  between operations  0.65 us (2%)
    pallas_call x1, Pallas kernels, fused_layer(): pl.pallas_call(functools.partial(layer_kernel, n_along, n_across), name='...  24.1 us
    unnamed x4, local copies, waits for them, and re-layouts  2.48 us

profile of v2, /device:TPU:0, one launch (start us, length us, event | category | flops | bytes accessed | tf_op | source)
XLA Modules:
  0.0 27.2 jit_solution(3313886394833914756)
XLA Ops:
  0.6 24.1 %mesh_layer.1 = (bf16[1024,256]{1,0:T(8,128)(2,1)}, f32[32,128]{1,0:T(8,128)}) custom-call(s32[4,8]{1,0:T(4,128)} %bitcast.7, s32[1,8]{1,0:T(1,128)} %bitcast.8, s32[1,128]{1,0:T(1,128)} %bitcast.9, s32[1,1024]{1,0:T(1,128)} %bitcast.6, bf16[1024,256]{1,0:T(8,128)(2,1)} %features_hbm.1, bf16[8,4,128,128]{3,2,1,0:T(8,128)(2,1)} %adj_hbm.1, ...), custom_call_target="tpu_custom_call" | custom-call | flops 939524096 | bytes 4194304 | tf_op jit(solution)/shard_map/mesh_layer/pallas_call | solution.py:536
  24.7 0.0 copy-start
  24.7 1.9 %copy.14 = bf16[1024,256]{1,0:T(8,128)(2,1)} copy(bf16[1024,256]{1,0:T(8,128)(2,1)} %get-tuple-element.8) | data formatting | bytes 1048576
  26.6 0.0 copy-done
  26.6 0.6 %copy.15 = f32[4096]{0:T(1024)} copy(f32[4096]{0:T(1024)S(1)} %bitcast.5) | data formatting | bytes 32768
Async XLA Ops:
  24.7 1.9 %copy-start = (f32[32,128]{1,0:T(8,128)S(1)}, f32[32,128]{1,0:T(8,128)}, u32[]{:S(2)}) copy-start(f32[32,128]{1,0:T(8,128)} %get-tuple-element.5) | copy-start | bytes 49156

commit v3 on v2

--- a/solution.py
+++ b/solution.py
@@ -274,14 +274,12 @@
             device_id_type=MESH,
         )
 
+    loads[1].wait()
+    bnd_column = jnp.broadcast_to(bnd_row[...].astype(f32), (tile, tile)).T[:, 0:1]
+    lanes = lax.broadcasted_iota(jnp.int32, (tile, nodes), 1)
+    rim_pick = (lanes == bnd_column.astype(jnp.int32)).astype(f32).astype(bf16)
     loads[0].wait()
-    for b in range(blocks):
-        x = features[b * tile : (b + 1) * tile, :].astype(f32)
-        sources[b] = normalize(x)[0].astype(bf16)
-    local_rows = sources[0:blocks].reshape(nodes, width)
-    loads[1].wait()
-    rim_pick = (lax.broadcasted_iota(jnp.int32, (nodes, tile), 0) == bnd_row[...]).astype(f32)
-    rim[...] = transposed_times(rim_pick.astype(bf16), local_rows).astype(bf16)
+    rim[...] = normalize(dot(rim_pick, features[...]))[0].astype(bf16)
 
     pl.semaphore_wait(barrier, n_across - 1 + n_along - 1)
 
@@ -306,6 +304,10 @@
         @pl.when(jnp.logical_not(has_source))
         def _(side=side):
             sources[blocks + side] = jnp.zeros((tile, width), bf16)
+
+    for b in range(blocks):
+        x = features[b * tile : (b + 1) * tile, :].astype(f32)
+        sources[b] = normalize(x)[0].astype(bf16)
 
     loads[2].wait()
     pool_pick = (
@@ -325,8 +327,7 @@
     w_first = w_update[0:width, :]
     w_second = w_update[width : 2 * width, :]
     w_joined[...] = dot(w_msg[...], w_second).astype(bf16)
-    for b in range(blocks):
-        pre[b * tile : (b + 1) * tile, :] = dot(sources[b], w_first)
+    pre[...] = dot(sources[0:blocks].reshape(nodes, width), w_first)
 
     for load in loads[6:9]:
         load.wait()
@@ -537,8 +538,8 @@
         functools.partial(layer_kernel, n_along, n_across),
         name="mesh_layer",
         out_shape=(
-            jax.ShapeDtypeStruct((nodes, width), bf16),
-            jax.ShapeDtypeStruct((chunk * width // 128, 128), f32),
+            vmem((nodes, width), bf16),
+            vmem((chunk * width // 128, 128), f32),
         ),
         in_specs=[hbm_spec] * 10,
         out_specs=(any_spec, vmem_spec),

time: 27.4 us -> 26.5 us (0.967)
  local copies, waits for them, and re-layouts: 2.48 us -> 1.4 us
    unnamed x4 -> x2, local copies, waits for them, and re-layouts: 2.48 us -> 1.4 us
where the time goes in v3:
time: 26.5 us; the launch traced here: 26.4 us
  Pallas kernels  24.3 us (92%)
  local copies, waits for them, and re-layouts  1.4 us (5%)
  between operations  0.64 us (2%)
    pallas_call x1, Pallas kernels, fused_layer(): pl.pallas_call(functools.partial(layer_kernel, n_along, n_across), name='...  24.3 us
    unnamed x2, local copies, waits for them, and re-layouts  1.4 us

profile of v3, /device:TPU:0, one launch (start us, length us, event | category | flops | bytes accessed | tf_op | source)
XLA Modules:
  0.0 26.4 jit_solution(3492650971345451919)
XLA Ops:
  0.6 24.3 %mesh_layer.1 = (bf16[1024,256]{1,0:T(8,128)(2,1)S(1)}, f32[32,128]{1,0:T(8,128)S(1)}) custom-call(s32[4,8]{1,0:T(4,128)} %bitcast.7, s32[1,8]{1,0:T(1,128)} %bitcast.8, s32[1,128]{1,0:T(1,128)} %bitcast.9, s32[1,1024]{1,0:T(1,128)} %bitcast.6, bf16[1024,256]{1,0:T(8,128)(2,1)} %features_hbm.1, bf16[8,4,128,128]{3,2,1,0:T(8,128)(2,1)} %adj_hbm.1, ...), custom_call_target="tpu_custom_call" | custom-call | flops 939524096 | bytes 4194304 | tf_op jit(solution)/shard_map/mesh_layer/pallas_call | solution.py:537
  25.0 0.8 %copy.14 = bf16[1024,256]{1,0:T(8,128)(2,1)} copy(bf16[1024,256]{1,0:T(8,128)(2,1)S(1)} %get-tuple-element.6) | data formatting | bytes 1048576
  25.8 0.6 %copy.15 = f32[4096]{0:T(1024)} copy(f32[4096]{0:T(1024)S(1)} %bitcast.5) | data formatting | bytes 32768

commit v4 on v3

--- a/solution.py
+++ b/solution.py
@@ -194,7 +194,7 @@
     slope,
     summed,
     summed_t,
-    update_delta,
+    picks,
     updated,
     pool_all,
     cot_all,
@@ -305,29 +305,36 @@
         def _(side=side):
             sources[blocks + side] = jnp.zeros((tile, width), bf16)
 
-    for b in range(blocks):
-        x = features[b * tile : (b + 1) * tile, :].astype(f32)
-        sources[b] = normalize(x)[0].astype(bf16)
-
-    loads[2].wait()
+    for load in loads[2:6]:
+        load.wait()
     pool_pick = (
         lax.broadcasted_iota(jnp.int32, (coarse_count, nodes), 0) == pool_row[...]
     ).astype(f32).astype(bf16)
-    loads[3].wait()
-    cot_all[c] = dot(pool_pick, cotangent[...])
+    picks[0:coarse_count, :] = pool_pick
+    picks[coarse_count : 2 * coarse_count, :] = pool_pick
+    w_first = w_update[0:width, :]
+    w_second = w_update[width : 2 * width, :]
+
+    def tile_rows(b, count=1):
+        size = count * tile
+        return pl.ds(pl.multiple_of(b * size, size), size)
+
+    def prepare(b, cot_part):
+        rows = tile_rows(b)
+        scaled = normalize(features[rows, :].astype(f32))[0].astype(bf16)
+        sources[b] = scaled
+        pre[rows, :] = dot(scaled, w_first)
+        return cot_part + dot(picks[0:coarse_count, rows], cotangent[rows, :])
+
+    zero = jnp.zeros((coarse_count, width), f32)
+    cot_all[c] = lax.fori_loop(0, blocks, prepare, zero)
     cot_copies = [
         remote(cot_all.at[c], cot_all.at[c], cot_send.at[d], cot_recv.at[c], (a, peer))
         for d, peer in enumerate(across_peers)
     ]
     for copy in cot_copies:
         copy.start()
-
-    loads[4].wait()
-    loads[5].wait()
-    w_first = w_update[0:width, :]
-    w_second = w_update[width : 2 * width, :]
     w_joined[...] = dot(w_msg[...], w_second).astype(bf16)
-    pre[...] = dot(sources[0:blocks].reshape(nodes, width), w_first)
 
     for load in loads[6:9]:
         load.wait()
@@ -337,14 +344,12 @@
         def _(side=side):
             halo(side, (a, c)).wait_recv()
 
-    pooled = jnp.zeros((coarse_count, width), f32)
-    for b in range(blocks):
-        rows = slice(b * tile, (b + 1) * tile)
+    def aggregate(b, pooled):
+        rows = tile_rows(b)
         gathered = jnp.concatenate([sources[adj_index[k, b]] for k in range(slots)], axis=0)
         weights = jnp.concatenate(
             [
-                adj[b, k]
-                * jnp.where(k < adj_count[0, b], 1.0, 0.0).astype(bf16)
+                adj[b, k] * jnp.where(k < adj_count[0, b], 1.0, 0.0).astype(bf16)
                 for k in range(slots)
             ],
             axis=1,
@@ -357,8 +362,10 @@
         h = features[rows, :].astype(f32) + v * s
         hidden[rows, :] = h
         high, low = split(h)
-        pick = pool_pick[:, rows]
-        pooled += dot(pick, high) + dot(pick, low)
+        pick = picks[0:coarse_count, rows]
+        return pooled + dot(pick, high) + dot(pick, low)
+
+    pooled = lax.fori_loop(0, blocks, aggregate, zero)
     pool_all[c] = pooled
     pool_copies = [
         remote(pool_all.at[c], pool_all.at[c], pool_send.at[d], pool_recv.at[c], (a, peer))
@@ -367,9 +374,11 @@
     for copy in pool_copies:
         copy.start()
 
-    for b in range(blocks):
-        rows = slice(b * tile, (b + 1) * tile)
-        summed_t[:, rows] = summed[rows, :].T
+    def transpose(b, carry):
+        summed_t[:, tile_rows(b)] = summed[tile_rows(b), :].T
+        return carry
+
+    lax.fori_loop(0, blocks, transpose, 0)
     loads[9].wait()
 
     for peer in across_peers:
@@ -406,14 +415,18 @@
     mean_two = jnp.mean(coarse_back * coarse_norm, axis=-1, keepdims=True)
     pooled_delta = inverse * (coarse_back - mean_one - coarse_norm * mean_two)
     delta_parts = jnp.concatenate(split(pooled_delta), axis=0)
-    twice_pick = jnp.concatenate([pool_pick, pool_pick], axis=0)
-
-    for b in range(blocks):
-        rows = slice(b * tile, (b + 1) * tile)
-        spread = transposed_times(twice_pick[:, rows], delta_parts)
+
+    total[...] = jnp.zeros(total.shape, f32)
+
+    def backward(b, carry):
+        rows = tile_rows(b, 2)
+        spread = transposed_times(picks[:, rows], delta_parts)
         hidden_delta = cotangent[rows, :].astype(f32) + spread
-        update_delta[rows, :] = (hidden_delta * slope[rows, :]).astype(bf16)
-    total[...] = dot(summed_t[...], update_delta[...])
+        update_delta = (hidden_delta * slope[rows, :]).astype(bf16)
+        total[...] += dot(summed_t[:, rows], update_delta)
+        return carry
+
+    lax.fori_loop(0, blocks // 2, backward, 0)
 
     for i in range(half):
         for j in range(n_across):
@@ -429,10 +442,13 @@
         for d, peer in enumerate(across_peers):
             send_part(i, d, peer).start()
 
-    for b in range(blocks):
-        rows = slice(b * tile, (b + 1) * tile)
-        spread = transposed_times(pool_pick[:, rows], coarse_out)
+    def update(b, carry):
+        rows = tile_rows(b)
+        spread = transposed_times(picks[0:coarse_count, rows], coarse_out)
         updated[rows, :] = (hidden[rows, :] + spread).astype(bf16)
+        return carry
+
+    lax.fori_loop(0, blocks, update, 0)
     store = pltpu.make_async_copy(updated, updated_hbm, out_sem.at[0])
     store.start()
 
@@ -562,7 +578,7 @@
             vmem((nodes, width), f32),
             vmem((nodes, width), bf16),
             vmem((width, nodes), bf16),
-            vmem((nodes, width), bf16),
+            vmem((2 * coarse_count, nodes), bf16),
             vmem((nodes, width), bf16),
             vmem((n_across, coarse_count, width), f32),
             vmem((n_across, coarse_count, width), f32),

time: 26.5 us -> 29 us (1.094)
  Pallas kernels: 24.3 us -> 26.8 us
    pallas_call x1, Pallas kernels: 24.3 us -> 26.8 us  [fused_layer(): pl.pallas_call(functools.partial(layer_kernel, n_along, n_across), name='...]
where the time goes in v4:
time: 29 us; the launch traced here: 28.9 us
  Pallas kernels  26.8 us (92%)
  local copies, waits for them, and re-layouts  1.4 us (5%)
  between operations  0.64 us (2%)
    pallas_call x1, Pallas kernels, fused_layer(): pl.pallas_call(functools.partial(layer_kernel, n_along, n_across), name='...  26.8 us
    unnamed x2, local copies, waits for them, and re-layouts  1.4 us

profile of v4, /device:TPU:0, one launch (start us, length us, event | category | flops | bytes accessed | tf_op | source)
XLA Modules:
  0.0 28.9 jit_solution(4815564988051692428)
XLA Ops:
  0.6 26.8 %mesh_layer.1 = (bf16[1024,256]{1,0:T(8,128)(2,1)S(1)}, f32[32,128]{1,0:T(8,128)S(1)}) custom-call(s32[4,8]{1,0:T(4,128)} %bitcast.7, s32[1,8]{1,0:T(1,128)} %bitcast.8, s32[1,128]{1,0:T(1,128)} %bitcast.9, s32[1,1024]{1,0:T(1,128)} %bitcast.6, bf16[1024,256]{1,0:T(8,128)(2,1)} %features_hbm.1, bf16[8,4,128,128]{3,2,1,0:T(8,128)(2,1)} %adj_hbm.1, ...), custom_call_target="tpu_custom_call" | custom-call | flops 939524096 | bytes 4194304 | tf_op jit(solution)/shard_map/mesh_layer/pallas_call | solution.py:553
  27.5 0.8 %copy.14 = bf16[1024,256]{1,0:T(8,128)(2,1)} copy(bf16[1024,256]{1,0:T(8,128)(2,1)S(1)} %get-tuple-element.6) | data formatting | bytes 1048576
  28.3 0.6 %copy.15 = f32[4096]{0:T(1024)} copy(f32[4096]{0:T(1024)S(1)} %bitcast.5) | data formatting | bytes 32768

commit v5 on v3

--- a/solution.py
+++ b/solution.py
@@ -195,6 +195,8 @@
     summed,
     summed_t,
     update_delta,
+    hidden_parts,
+    pick_rows,
     updated,
     pool_all,
     cot_all,
@@ -258,11 +260,17 @@
 
     barrier = pltpu.get_barrier_semaphore()
     across_peers = [lax.rem(c + d, n_across) for d in range(1, n_across)]
+    z, x = lax.div(a, 2), lax.rem(a, 2)
+    layers, owners = n_along // 2, half // 2
+    group = 2 * n_across
+    place = x * n_across + c
+    places = [lax.rem(place + d, group) for d in range(1, group)]
+    group_peers = [(2 * z + lax.div(q, n_across), lax.rem(q, n_across)) for q in places]
+    layer_peers = [lax.rem(z + d, layers) for d in range(1, layers)]
     along_peers = [lax.rem(a + d, n_along) for d in range(1, n_along)]
-    for peer in across_peers:
-        pl.semaphore_signal(barrier, inc=1, device_id=(a, peer), device_id_type=MESH)
-    for peer in along_peers:
-        pl.semaphore_signal(barrier, inc=1, device_id=(peer, c), device_id_type=MESH)
+    greeted = group_peers + [(2 * peer + i, c) for peer in layer_peers for i in range(2)]
+    for device in greeted:
+        pl.semaphore_signal(barrier, inc=1, device_id=device, device_id_type=MESH)
 
     def remote(source, target, send, recv, device):
         return pltpu.make_async_remote_copy(
@@ -281,7 +289,7 @@
     loads[0].wait()
     rim[...] = normalize(dot(rim_pick, features[...]))[0].astype(bf16)
 
-    pl.semaphore_wait(barrier, n_across - 1 + n_along - 1)
+    pl.semaphore_wait(barrier, len(greeted))
 
     sides = (
         (a < n_along - 1, (a + 1, c), a > 0),
@@ -306,13 +314,14 @@
             sources[blocks + side] = jnp.zeros((tile, width), bf16)
 
     for b in range(blocks):
-        x = features[b * tile : (b + 1) * tile, :].astype(f32)
-        sources[b] = normalize(x)[0].astype(bf16)
+        block = features[b * tile : (b + 1) * tile, :].astype(f32)
+        sources[b] = normalize(block)[0].astype(bf16)
 
     loads[2].wait()
     pool_pick = (
         lax.broadcasted_iota(jnp.int32, (coarse_count, nodes), 0) == pool_row[...]
     ).astype(f32).astype(bf16)
+    pick_rows[...] = jnp.concatenate([pool_pick, pool_pick], axis=0).astype(f32).T.astype(bf16)
     loads[3].wait()
     cot_all[c] = dot(pool_pick, cotangent[...])
     cot_copies = [
@@ -337,28 +346,25 @@
         def _(side=side):
             halo(side, (a, c)).wait_recv()
 
-    pooled = jnp.zeros((coarse_count, width), f32)
     for b in range(blocks):
-        rows = slice(b * tile, (b + 1) * tile)
         gathered = jnp.concatenate([sources[adj_index[k, b]] for k in range(slots)], axis=0)
         weights = jnp.concatenate(
             [
-                adj[b, k]
-                * jnp.where(k < adj_count[0, b], 1.0, 0.0).astype(bf16)
+                adj[b, k] * jnp.where(k < adj_count[0, b], 1.0, 0.0).astype(bf16)
                 for k in range(slots)
             ],
             axis=1,
         )
-        block_sum = dot(weights, gathered).astype(bf16)
-        summed[rows, :] = block_sum
-        v = pre[rows, :] + dot(block_sum, w_joined[...])
+        summed[b * tile : (b + 1) * tile, :] = dot(weights, gathered).astype(bf16)
+    for b in range(0, blocks, 2):
+        rows = slice(b * tile, (b + 2) * tile)
+        v = pre[rows, :] + dot(summed[rows, :], w_joined[...])
         s = sigmoid(v)
         slope[rows, :] = s * (1.0 + v * (1.0 - s))
         h = features[rows, :].astype(f32) + v * s
         hidden[rows, :] = h
-        high, low = split(h)
-        pick = pool_pick[:, rows]
-        pooled += dot(pick, high) + dot(pick, low)
+        hidden_parts[0, rows, :], hidden_parts[1, rows, :] = split(h)
+    pooled = dot(pool_pick, hidden_parts[0]) + dot(pool_pick, hidden_parts[1])
     pool_all[c] = pooled
     pool_copies = [
         remote(pool_all.at[c], pool_all.at[c], pool_send.at[d], pool_recv.at[c], (a, peer))
@@ -406,55 +412,56 @@
     mean_two = jnp.mean(coarse_back * coarse_norm, axis=-1, keepdims=True)
     pooled_delta = inverse * (coarse_back - mean_one - coarse_norm * mean_two)
     delta_parts = jnp.concatenate(split(pooled_delta), axis=0)
-    twice_pick = jnp.concatenate([pool_pick, pool_pick], axis=0)
+    for b in range(0, blocks, 2):
+        rows = slice(b * tile, (b + 2) * tile)
+        hidden_delta = cotangent[rows, :].astype(f32) + dot(pick_rows[rows, :], delta_parts)
+        update_delta[rows, :] = (hidden_delta * slope[rows, :]).astype(bf16)
+    total[...] = dot(summed_t[...], update_delta[...])
+
+    for q in range(group):
+        for i in range(owners):
+            start = ((2 * i + q // n_across) * n_across + q % n_across) * chunk
+            part[q, i] = total[start : start + chunk, :].astype(bf16)
+
+    def send_part(i, d):
+        return remote(
+            part.at[places[d], i],
+            part_all.at[place, i],
+            part_send.at[d, i],
+            part_recv.at[place, i],
+            group_peers[d],
+        )
+
+    for i in range(owners):
+        for d in range(group - 1):
+            send_part(i, d).start()
 
     for b in range(blocks):
         rows = slice(b * tile, (b + 1) * tile)
-        spread = transposed_times(twice_pick[:, rows], delta_parts)
-        hidden_delta = cotangent[rows, :].astype(f32) + spread
-        update_delta[rows, :] = (hidden_delta * slope[rows, :]).astype(bf16)
-    total[...] = dot(summed_t[...], update_delta[...])
-
-    for i in range(half):
-        for j in range(n_across):
-            start = (i * n_across + j) * chunk
-            part[j, i] = total[start : start + chunk, :].astype(bf16)
-
-    def send_part(i, d, peer):
-        return remote(
-            part.at[peer, i], part_all.at[c, i], part_send.at[d, i], part_recv.at[c, i], (a, peer)
-        )
-
-    for i in reversed(range(half)):
-        for d, peer in enumerate(across_peers):
-            send_part(i, d, peer).start()
-
-    for b in range(blocks):
-        rows = slice(b * tile, (b + 1) * tile)
-        spread = transposed_times(pool_pick[:, rows], coarse_out)
+        spread = dot(pick_rows[rows, 0:coarse_count], coarse_out)
         updated[rows, :] = (hidden[rows, :] + spread).astype(bf16)
     store = pltpu.make_async_copy(updated, updated_hbm, out_sem.at[0])
     store.start()
 
     def send_second(i):
         return remote(
-            second.at[i], second_all.at[a], second_send.at[i], second_recv.at[a], (i, c)
+            second.at[i], second_all.at[z], second_send.at[i], second_recv.at[z], (2 * i + x, c)
         )
 
-    for i in reversed(range(half)):
-        start = pl.multiple_of((i * n_across + c) * chunk, chunk)
+    for i in range(owners):
+        start = pl.multiple_of(((2 * i + x) * n_across + c) * chunk, chunk)
         chunk_sum = total[pl.ds(start, chunk), :]
-        for peer in across_peers:
+        for q in places:
             remote(
-                part.at[peer, i], part_all.at[peer, i], part_send.at[0, i], part_recv.at[peer, i], (a, c)
+                part.at[q, i], part_all.at[q, i], part_send.at[0, i], part_recv.at[q, i], (a, c)
             ).wait_recv()
-            chunk_sum = chunk_sum + part_all[peer, i].astype(f32)
-
-        @pl.when(a == i)
+            chunk_sum = chunk_sum + part_all[q, i].astype(f32)
+
+        @pl.when(z == i)
         def _(chunk_sum=chunk_sum):
             own_chunk[...] = chunk_sum
 
-        @pl.when(a != i)
+        @pl.when(z != i)
         def _(chunk_sum=chunk_sum, i=i):
             second[i] = chunk_sum.astype(bf16)
             send_second(i).start()
@@ -462,7 +469,7 @@
     @pl.when(a < half)
     def _():
         chunk_sum = own_chunk[...]
-        for peer in along_peers:
+        for peer in layer_peers:
             remote(
                 second.at[0], second_all.at[peer], second_send.at[0], second_recv.at[peer], (a, c)
             ).wait_recv()
@@ -499,11 +506,11 @@
         def _(target=target):
             send_pack(target).wait_send()
 
-    for i in range(half):
-        for d, peer in enumerate(across_peers):
-            send_part(i, d, peer).wait_send()
-
-        @pl.when(a != i)
+    for i in range(owners):
+        for d in range(group - 1):
+            send_part(i, d).wait_send()
+
+        @pl.when(z != i)
         def _(i=i):
             send_second(i).wait_send()
 
@@ -563,6 +570,8 @@
             vmem((nodes, width), bf16),
             vmem((width, nodes), bf16),
             vmem((nodes, width), bf16),
+            vmem((2, nodes, width), bf16),
+            vmem((nodes, 2 * coarse_count), bf16),
             vmem((nodes, width), bf16),
             vmem((n_across, coarse_count, width), f32),
             vmem((n_across, coarse_count, width), f32),
@@ -570,10 +579,10 @@
             vmem((n_along, 2 * coarse_count, width), bf16),
             vmem((width, width), f32),
             vmem((width, width), f32),
-            vmem((n_across, half, chunk, width), bf16),
-            vmem((n_across, half, chunk, width), bf16),
-            vmem((half, chunk, width), bf16),
-            vmem((n_along, chunk, width), bf16),
+            vmem((2 * n_across, half // 2, chunk, width), bf16),
+            vmem((2 * n_across, half // 2, chunk, width), bf16),
+            vmem((half // 2, chunk, width), bf16),
+            vmem((n_along // 2, chunk, width), bf16),
             vmem((chunk, width), f32),
             dma((10,)),
             dma((1,)),
@@ -585,10 +594,10 @@
             dma((n_across,)),
             dma((half,)),
             dma((n_along,)),
-            dma((n_across, half)),
-            dma((n_across, half)),
-            dma((half,)),
-            dma((n_along,)),
+            dma((2 * n_across, half // 2)),
+            dma((2 * n_across, half // 2)),
+            dma((half // 2,)),
+            dma((n_along // 2,)),
         ],
         compiler_params=pltpu.CompilerParams(
             collective_id=0, has_side_effects=True, vmem_limit_bytes=60 * 2**20
@@ -617,7 +626,7 @@
     n_along, n_across = axes["along"], axes["across"]
     width = features.shape[1]
     chunk = 2 * width // (n_along * n_across)
-    if n_along % 2 == 0 and chunk and chunk % 16 == 0:
+    if n_along % 4 == 0 and chunk and chunk % 16 == 0:
         return fused_layer(n_along, n_across, chunk, features, adj_tiles, *others)
     return plain_layer(features, adj_tiles, *others)
 

time: 26.5 us -> 24.6 us (0.928)
  Pallas kernels: 24.3 us -> 22.4 us
    pallas_call x1, Pallas kernels: 24.3 us -> 22.4 us  [fused_layer(): pl.pallas_call(functools.partial(layer_kernel, n_along, n_across), name='...]
where the time goes in v5:
time: 24.6 us; the launch traced here: 24.4 us
  Pallas kernels  22.4 us (91%)
  local copies, waits for them, and re-layouts  1.4 us (6%)
  between operations  0.64 us (3%)
    pallas_call x1, Pallas kernels, fused_layer(): pl.pallas_call(functools.partial(layer_kernel, n_along, n_across), name='...  22.4 us
    unnamed x2, local copies, waits for them, and re-layouts  1.4 us

profile of v5, /device:TPU:0, one launch (start us, length us, event | category | flops | bytes accessed | tf_op | source)
XLA Modules:
  0.0 24.4 jit_solution(15164707526823498888)
XLA Ops:
  0.6 22.4 %mesh_layer.1 = (bf16[1024,256]{1,0:T(8,128)(2,1)S(1)}, f32[32,128]{1,0:T(8,128)S(1)}) custom-call(s32[4,8]{1,0:T(4,128)} %bitcast.7, s32[1,8]{1,0:T(1,128)} %bitcast.8, s32[1,128]{1,0:T(1,128)} %bitcast.9, s32[1,1024]{1,0:T(1,128)} %bitcast.6, bf16[1024,256]{1,0:T(8,128)(2,1)} %features_hbm.1, bf16[8,4,128,128]{3,2,1,0:T(8,128)(2,1)} %adj_hbm.1, ...), custom_call_target="tpu_custom_call" | custom-call | flops 939524096 | bytes 4194304 | tf_op jit(solution)/shard_map/mesh_layer/pallas_call | solution.py:544
  23.0 0.8 %copy.14 = bf16[1024,256]{1,0:T(8,128)(2,1)} copy(bf16[1024,256]{1,0:T(8,128)(2,1)S(1)} %get-tuple-element.6) | data formatting | bytes 1048576
  23.8 0.6 %copy.15 = f32[4096]{0:T(1024)} copy(f32[4096]{0:T(1024)S(1)} %bitcast.5) | data formatting | bytes 32768

commit v6 on v5

--- a/solution.py
+++ b/solution.py
@@ -255,7 +255,7 @@
             )
         )
     ]
-    for load in loads:
+    for load in loads[0:2]:
         load.start()
 
     barrier = pltpu.get_barrier_semaphore()
@@ -271,6 +271,8 @@
     greeted = group_peers + [(2 * peer + i, c) for peer in layer_peers for i in range(2)]
     for device in greeted:
         pl.semaphore_signal(barrier, inc=1, device_id=device, device_id_type=MESH)
+    for load in loads[2:]:
+        load.start()
 
     def remote(source, target, send, recv, device):
         return pltpu.make_async_remote_copy(
@@ -321,16 +323,6 @@
     pool_pick = (
         lax.broadcasted_iota(jnp.int32, (coarse_count, nodes), 0) == pool_row[...]
     ).astype(f32).astype(bf16)
-    pick_rows[...] = jnp.concatenate([pool_pick, pool_pick], axis=0).astype(f32).T.astype(bf16)
-    loads[3].wait()
-    cot_all[c] = dot(pool_pick, cotangent[...])
-    cot_copies = [
-        remote(cot_all.at[c], cot_all.at[c], cot_send.at[d], cot_recv.at[c], (a, peer))
-        for d, peer in enumerate(across_peers)
-    ]
-    for copy in cot_copies:
-        copy.start()
-
     loads[4].wait()
     loads[5].wait()
     w_first = w_update[0:width, :]
@@ -373,6 +365,16 @@
     for copy in pool_copies:
         copy.start()
 
+    loads[3].wait()
+    cot_all[c] = dot(pool_pick, cotangent[...])
+    cot_copies = [
+        remote(cot_all.at[c], cot_all.at[c], cot_send.at[d], cot_recv.at[c], (a, peer))
+        for d, peer in enumerate(across_peers)
+    ]
+    for copy in cot_copies:
+        copy.start()
+
+    pick_rows[...] = jnp.concatenate([pool_pick, pool_pick], axis=0).astype(f32).T.astype(bf16)
     for b in range(blocks):
         rows = slice(b * tile, (b + 1) * tile)
         summed_t[:, rows] = summed[rows, :].T
@@ -380,20 +382,24 @@
 
     for peer in across_peers:
         remote(
-            cot_all.at[peer], cot_all.at[peer], cot_send.at[0], cot_recv.at[peer], (a, c)
-        ).wait_recv()
-        remote(
             pool_all.at[peer], pool_all.at[peer], pool_send.at[0], pool_recv.at[peer], (a, c)
         ).wait_recv()
-    pooled, coarse_cot = pool_all[0], cot_all[0]
+    pooled = pool_all[0]
     for i in range(1, n_across):
-        pooled, coarse_cot = pooled + pool_all[i], coarse_cot + cot_all[i]
+        pooled = pooled + pool_all[i]
 
     coarse_norm, inverse = normalize(pooled)
     coarse = coarse_norm.astype(bf16)
     coarse_pre = dot(coarse, w_coarse[...])
     s = sigmoid(coarse_pre)
     coarse_out = (coarse_pre * s).astype(bf16)
+    for peer in across_peers:
+        remote(
+            cot_all.at[peer], cot_all.at[peer], cot_send.at[0], cot_recv.at[peer], (a, c)
+        ).wait_recv()
+    coarse_cot = cot_all[0]
+    for i in range(1, n_across):
+        coarse_cot = coarse_cot + cot_all[i]
     coarse_delta = (coarse_cot * (s * (1.0 + coarse_pre * (1.0 - s)))).astype(bf16)
     pack[0:coarse_count, :] = coarse
     pack[coarse_count : 2 * coarse_count, :] = coarse_delta
@@ -515,6 +521,17 @@
             send_second(i).wait_send()
 
     store.wait()
+
+
+def store_kernel(updated, grads, updated_hbm, grads_hbm, sem):
+    copies = [
+        pltpu.make_async_copy(updated, updated_hbm, sem.at[0]),
+        pltpu.make_async_copy(grads, grads_hbm, sem.at[1]),
+    ]
+    for copy in copies:
+        copy.start()
+    for copy in copies:
+        copy.wait()
 
 
 def fused_layer(
@@ -619,6 +636,17 @@
         w_coarse,
         cotangent,
     )
+    updated, grads = pl.pallas_call(
+        store_kernel,
+        name="store_results",
+        out_shape=(
+            jax.ShapeDtypeStruct(updated.shape, bf16),
+            jax.ShapeDtypeStruct(grads.shape, f32),
+        ),
+        in_specs=[any_spec] * 2,
+        out_specs=(hbm_spec, hbm_spec),
+        scratch_shapes=[dma((2,))],
+    )(updated, grads)
     return updated, grads.reshape(-1)
 
 

time: 24.6 us -> 42.1 us (1.71)
  Pallas kernels: 22.4 us -> 40 us
    pallas_call x0 -> x1, Pallas kernels: none -> 17.5 us  [fused_layer(): pl.pallas_call(store_kernel, name='store_results', out_shape=(jax.ShapeDt...]
    unnamed x2 -> x4, local copies, waits for them, and re-layouts: 1.4 us -> 1.38 us
where the time goes in v6:
time: 42.1 us; the launch traced here: 42 us
  Pallas kernels  40 us (95%)
  local copies, waits for them, and re-layouts  1.38 us (3%)
  between operations  0.65 us (2%)
    pallas_call x1, Pallas kernels, fused_layer(): pl.pallas_call(functools.partial(layer_kernel, n_along, n_across), name='...  22.5 us
    pallas_call x1, Pallas kernels, fused_layer(): pl.pallas_call(store_kernel, name='store_results', out_shape=(jax.ShapeDt...  17.5 us
    unnamed x4, local copies, waits for them, and re-layouts  1.38 us

profile of v6, /device:TPU:0, one launch (start us, length us, event | category | flops | bytes accessed | tf_op | source)
XLA Modules:
  0.0 42.0 jit_solution(2317779048192951361)
XLA Ops:
  0.6 22.5 %mesh_layer.1 = (bf16[1024,256]{1,0:T(8,128)(2,1)S(1)}, f32[32,128]{1,0:T(8,128)S(1)}) custom-call(s32[4,8]{1,0:T(4,128)} %bitcast.7, s32[1,8]{1,0:T(1,128)} %bitcast.8, s32[1,128]{1,0:T(1,128)} %bitcast.9, s32[1,1024]{1,0:T(1,128)} %bitcast.6, bf16[1024,256]{1,0:T(8,128)(2,1)} %features_hbm.1, bf16[8,4,128,128]{3,2,1,0:T(8,128)(2,1)} %adj_hbm.1, ...), custom_call_target="tpu_custom_call" | custom-call | flops 939524096 | bytes 4194304 | tf_op jit(solution)/shard_map/mesh_layer/pallas_call | solution.py:561
  23.1 0.0 copy-start
  23.1 0.8 %copy-done = bf16[1024,256]{1,0:T(8,128)(2,1)} copy-done((bf16[1024,256]{1,0:T(8,128)(2,1)}, bf16[1024,256]{1,0:T(8,128)(2,1)S(1)}, u32[]{:S(2)}) %copy-start) | copy-done | bytes 524312
  23.9 0.0 copy-start.1
  23.9 0.6 %copy-done.1 = f32[32,128]{1,0:T(8,128)} copy-done((f32[32,128]{1,0:T(8,128)}, f32[32,128]{1,0:T(8,128)S(1)}, u32[]{:S(2)}) %copy-start.1) | copy-done | bytes 16408
  24.5 17.5 %store_results.1 = (bf16[1024,256]{1,0:T(8,128)(2,1)}, f32[32,128]{1,0:T(8,128)}) custom-call(bf16[1024,256]{1,0:T(8,128)(2,1)} %copy-done, f32[32,128]{1,0:T(8,128)} %copy-done.1), custom_call_target="tpu_custom_call" | custom-call | tf_op jit(solution)/shard_map/store_results/pallas_call | solution.py:639
Async XLA Ops:
  23.1 0.8 %copy-start = (bf16[1024,256]{1,0:T(8,128)(2,1)}, bf16[1024,256]{1,0:T(8,128)(2,1)S(1)}, u32[]{:S(2)}) copy-start(bf16[1024,256]{1,0:T(8,128)(2,1)S(1)} %get-tuple-element.6.updated) | copy-start | bytes 1572868
  23.9 0.6 %copy-start.1 = (f32[32,128]{1,0:T(8,128)}, f32[32,128]{1,0:T(8,128)S(1)}, u32[]{:S(2)}) copy-start(f32[32,128]{1,0:T(8,128)S(1)} %get-tuple-element.7.grads) | copy-start | bytes 49156
